TPU v7x, 512 devices: a whole 4x8x8 slice. The times are simulated.
512 devices in a mesh: elec: 64 (over z, x, core), cell: 8 (over y).
Axes of the slice: x: 4, y: 8, z: 8, core: 2. Of those that a mesh axis runs over, the one named last changes fastest.
Arguments:
- fields: bfloat16 [2, 3, 512, 65536], P(None, None, 'elec', 'cell'), may hold values from -6 to 6
- residual: float32 [65536, 8, 2], P(('elec', 'cell')), may hold values from -0.0024414062 to 0.0024414062
- quad_group: int32 [65536, 1], P(('elec', 'cell')), may hold values from 0 to 63; in each aligned block of 128 rows (0 to 127, 128 to 255, ...) at most 4 rows name the same one
- offsets: int32 [65536, 3], P(('elec', 'cell')), may hold values from 0 to 7
- b_step: int32 [65536, 1], P(('elec', 'cell')), may hold values from 1 to 7
- sides: int32 [65536, 2], P(('elec', 'cell')), may hold values from -1 to 1, as said below
Outputs:
- gradient: float32 [8, 2, 8, 8192], P(None, None, 'cell', 'elec')
Inputs may be any that keep to these rules, and one draw needn't show every extreme that they name: `quad_group`: within the quadrupoles of one device (aligned blocks of 128 rows), no group is named more than 4 times, a bound that some block reaches. In every quadrupole at least one of the two sides is -1.
All inputs are finite; a program needn't handle non-finite values.
Results may differ from a plain program's by a relative error of at most 0.0029.
Values may be sent and summed in bfloat16 or wider, within the bound.
A program may use at most 128 MiB of HBM per device.

v0:
```python
import math

import jax
import jax.numpy as jnp
from jax import lax
from jax.sharding import PartitionSpec as P


def extended(block, sides, width):
    for axis, dim in sides:
        count = lax.axis_size(axis)
        forward = [(i, i + 1) for i in range(count - 1)]
        backward = [(target, source) for source, target in forward]
        low = lax.ppermute(
            lax.slice_in_dim(block, block.shape[dim] - width, None, axis=dim), axis, forward
        )
        high = lax.ppermute(lax.slice_in_dim(block, 0, width, axis=dim), axis, backward)
        block = jnp.concatenate([low, block, high], axis=dim)
    return block


def locate(quad_group, offsets, b_step, sides, groups, per_group):
    owner = quad_group[:, 0]
    source_a = offsets[:, 0]
    source_b = (source_a + b_step[:, 0]) % per_group
    group_m = jnp.clip(owner + sides[:, 0], 0, groups - 1)
    group_n = jnp.clip(owner + sides[:, 1], 0, groups - 1)
    column_m = (group_m - owner + 1) * per_group + offsets[:, 1]
    column_n = (group_n - owner + 1) * per_group + offsets[:, 2]
    return (owner, source_a, source_b, column_m, column_n)


def decode(packed, per_group):
    source_a = packed % per_group
    remaining = packed // per_group
    source_b = remaining % per_group
    remaining = remaining // per_group
    column_m = remaining % (3 * per_group)
    remaining = remaining // (3 * per_group)
    column_n = remaining % (3 * per_group)
    owner = remaining // (3 * per_group)
    return (owner, source_a, source_b, column_m, column_n)


def signed_pair(plus_index, minus_index, extent):
    positions = jnp.arange(extent, dtype=jnp.int32)[None, :]
    return (positions == plus_index[:, None]).astype(jnp.float32) - (
        positions == minus_index[:, None]
    ).astype(jnp.float32)


def band_terms(row_diff, values, col_diff):
    row_count = row_diff.shape[0]
    row_step = math.gcd(row_count, 2048)
    flat_width = values.shape[1] * col_diff.shape[1]

    def add_block(number, accumulated):
        rows_part = lax.dynamic_slice_in_dim(row_diff, number * row_step, row_step, 0)
        values_part = lax.dynamic_slice_in_dim(values, number * row_step, row_step, 0)
        cols_part = lax.dynamic_slice_in_dim(col_diff, number * row_step, row_step, 0)
        outer = (values_part[:, :, None] * cols_part[:, None, :]).reshape(row_step, flat_width)
        return accumulated + jnp.dot(
            rows_part.T, outer, precision=lax.Precision.HIGHEST, preferred_element_type=jnp.float32
        )

    start_value = jnp.zeros((row_diff.shape[1], flat_width), jnp.float32)
    return lax.fori_loop(0, row_count // row_step, add_block, start_value)


def stack_rows(sources):
    real_rows = sources[:, 0]
    imag_rows = sources[:, 1]
    upper_half = jnp.stack([real_rows, imag_rows], axis=2)
    lower_half = jnp.stack([imag_rows, -imag_rows * 0 - real_rows], axis=2)
    return jnp.stack([upper_half, lower_half], axis=0)


def correlate_local(fields, pairings, frames):
    cell_count = fields.shape[3]
    block_cells = math.gcd(cell_count, 2048)

    def accumulate(number, accumulated):
        first_cell = number * block_cells
        middle = lax.dynamic_slice_in_dim(fields, first_cell, block_cells, 3).astype(jnp.float32)
        adjoint = None
        for row_blocks, source_window in pairings:
            window_part = lax.dynamic_slice_in_dim(source_window, first_cell, block_cells, 3)
            term = jnp.einsum(
                "oteij,icjk->otcek", row_blocks, window_part, preferred_element_type=jnp.float32
            )
            adjoint = term
        real_part = -jnp.einsum("icek,itcek->tk", middle, adjoint)
        imag_part = -(
            jnp.einsum("cek,tcek->tk", middle[0], adjoint[1])
            - jnp.einsum("cek,tcek->tk", middle[1], adjoint[0])
        )
        return lax.dynamic_update_slice_in_dim(
            accumulated, jnp.stack([real_part, imag_part], axis=1), first_cell, 2
        )

    start_value = jnp.zeros((frames, 2, cell_count), jnp.float32)
    return lax.fori_loop(0, cell_count // block_cells, accumulate, start_value)


def local(fields, residual, quad_group, offsets, b_step, sides):
    groups = lax.axis_size("elec")
    own_group = lax.axis_index("elec")
    per_group = fields.shape[2]
    frames = residual.shape[1]
    local_count = residual.shape[0]
    window_width = 3 * per_group
    owner, source_a, source_b, column_m, column_n = locate(
        quad_group, offsets, b_step, sides, groups, per_group
    )
    packed = source_a + per_group * (
        source_b + per_group * (column_m + window_width * (column_n + window_width * owner))
    )
    values = residual.reshape(local_count, 2 * frames)
    every_value, every_packed = (
        lax.all_gather(values, ("elec", "cell"), axis=0, tiled=True),
        lax.all_gather(packed, ("elec", "cell"), axis=0, tiled=True),
    )
    owner_all, source_a_all, source_b_all, column_m_all, column_n_all = decode(
        every_packed, per_group
    )
    mine_mask = (owner_all == own_group).astype(jnp.float32)
    row_diff = signed_pair(source_a_all, source_b_all, per_group) * mine_mask[:, None]
    band_rows = band_terms(
        row_diff, every_value, signed_pair(column_m_all, column_n_all, window_width)
    )
    sources = jnp.transpose(
        band_rows.reshape(per_group, frames, 2, window_width), (1, 2, 0, 3)
    ).astype(jnp.bfloat16)
    window = extended(fields, (("elec", 2),), per_group)
    summed = correlate_local(fields, [(stack_rows(sources), window)], frames)
    cell_share = lax.psum_scatter(summed, "elec", scatter_dimension=2, tiled=True)
    return cell_share.reshape(frames, 2, 1, cell_share.shape[2])


def solution(mesh):
    return jax.shard_map(
        local,
        mesh=mesh,
        in_specs=(
            P(None, None, "elec", "cell"),
            P(("elec", "cell"), None, None),
            P(("elec", "cell"), None),
            P(("elec", "cell"), None),
            P(("elec", "cell"), None),
            P(("elec", "cell"), None),
        ),
        out_specs=P(None, None, "cell", "elec"),
        check_vma=False,
    )
```

profile of v0, /device:TPU:1, one launch (start us, length us, event | category | flops | bytes accessed | tf_op | source)
XLA Modules:
  0.0 525.1 jit_solution(865773029018241539)
XLA Ops:
  6.5 1.2 copy.17
  7.7 8.8 %collective-permute-start.1 = (bf16[2,3,8,8192]{3,2,0,1:T(8,128)(2,1)S(1)}, bf16[2,3,8,8192]{3,2,0,1:T(8,128)(2,1)S(1)}, u32[]{:S(2)}, u32[]{:S(2)}) collective-permute-start(bf16[2,3,8,8192]{3,2,0,1:T(8,128)(2,1)S(1)} %copy.17), channel_id=1, source_target_pairs={{8,0},{16,8},{24,16},{32,24},{40,32},{48,40},{56,48},{64,56},{72,6... | collective-permute-start | bytes 2359304 | tf_op jit(solution)/shard_map/ppermute | solution.py:17
  16.5 1.9 collective-permute-start
  19.3 64.8 %all-gather = s32[512,1,128]{2,1,0:T(1,128)S(1)} all-gather(s32[1,1,128]{2,1,0:T(1,128)S(1)} %fusion.31), channel_id=1, replica_groups=mesh['elec'=64,'cell'=8] {'elec','cell'}, dimensions={0}, use_global_device_ids=true | all-gather | bytes 262656 | tf_op jit(solution)/shard_map/all_gather | solution.py:121
  85.5 3.7 convert_subtract_fusion
  89.1 1.7 subtract_multiply_fusion
  91.8 1.6 pad_maximum_fusion
  93.4 46.4 %all-gather.3.cloned.1.call-done = f32[65536,16]{0,1:T(8,128)} async-done(((f32[128,16]{0,1:T(8,128)}), f32[65536,16]{0,1:T(8,128)}) %all-gather.3.cloned.1.call-update) | async-done | bytes 4194320 | tf_op jit(solution)/shard_map/all_gather | solution.py:120
  139.8 184.3 %while.28 = (s32[]{:T(128)}, f32[8,384]{1,0:T(8,128)S(1)}, f32[65536,8]{0,1:T(8,128)}, f32[65536,16]{0,1:T(8,128)}, f32[65536,24]{0,1:T(8,128)}, /*index=5*/s32[]{:T(128)}, s32[]{:T(128)}, s32[]{:T(128)}, s32[]{:T(128)}) while((s32[]{:T(128)}, f32[8,384]{1,0:T(8,128)S(1)}, f32[65536,8]{0,1:T(8,128)}, f32[65536,16]{0,1:T(8,128)}, ...), condition=%wide.region_1.2_spmd.clone, body=%wide.region_0.1_spmd.clone.sunk | while | flops 76290056 | bytes 7364777 | solution.py:67
  142.0 3.5 convolution_add_fusion.2
  146.4 0.9 constant_dynamic-slice_fusion.4
  147.8 3.5 convolution_add_fusion.2
  152.2 0.9 constant_dynamic-slice_fusion.4
  153.5 3.5 convolution_add_fusion.2
  159.3 3.5 convolution_add_fusion.2
  163.7 0.9 constant_dynamic-slice_fusion.4
  165.0 3.5 convolution_add_fusion.2
  169.5 0.9 constant_dynamic-slice_fusion.4
  170.8 3.5 convolution_add_fusion.2
  175.3 0.9 constant_dynamic-slice_fusion.4
  176.6 3.5 convolution_add_fusion.2
  181.0 0.9 constant_dynamic-slice_fusion.4
  182.3 3.5 convolution_add_fusion.2
  188.1 3.5 convolution_add_fusion.2
  192.5 0.9 constant_dynamic-slice_fusion.4
  193.9 3.5 convolution_add_fusion.2
  198.3 0.9 constant_dynamic-slice_fusion.4
  199.6 3.5 convolution_add_fusion.2
  205.4 3.5 convolution_add_fusion.2
  209.8 0.9 constant_dynamic-slice_fusion.4
  211.1 3.5 convolution_add_fusion.2
  215.6 0.9 constant_dynamic-slice_fusion.4
  216.9 3.5 convolution_add_fusion.2
  222.7 3.5 convolution_add_fusion.2
  227.1 0.9 constant_dynamic-slice_fusion.4
  228.4 3.5 convolution_add_fusion.2
  232.9 0.9 constant_dynamic-slice_fusion.4
  234.2 3.5 convolution_add_fusion.2
  238.6 0.9 constant_dynamic-slice_fusion.4
  239.9 3.5 convolution_add_fusion.2
  244.4 0.9 constant_dynamic-slice_fusion.4
  245.7 3.5 convolution_add_fusion.2
  251.5 3.5 convolution_add_fusion.2
  255.9 0.9 constant_dynamic-slice_fusion.4
  257.2 3.5 convolution_add_fusion.2
  261.7 0.9 constant_dynamic-slice_fusion.4
  263.0 3.5 convolution_add_fusion.2
  268.7 3.5 convolution_add_fusion.2
  273.2 0.9 constant_dynamic-slice_fusion.4
  274.5 3.5 convolution_add_fusion.2
  280.3 3.5 convolution_add_fusion.2
  286.0 3.5 convolution_add_fusion.2
  291.8 3.5 convolution_add_fusion.2
  297.6 3.5 convolution_add_fusion.2
  303.3 3.5 convolution_add_fusion.2
  309.1 3.5 convolution_add_fusion.2
  314.8 3.5 convolution_add_fusion.2
  320.6 3.5 convolution_add_fusion.2
  324.3 1.0 broadcast_in_dim.8
  325.3 8.8 %while.27 = (s32[]{:T(128)}, f32[8,2,8192]{2,1,0:T(2,128)}, bf16[2,3,24,8192]{3,2,0,1:T(8,128)(2,1)S(1)}, bf16[2,8,8,2,24]{4,2,3,1,0:T(8,128)(2,1)S(1)}, bf16[2,...) while((s32[]{:T(128)}, f32[8,2,8192]{2,1,0:T(2,128)}, ...), condition=%wide.region_3.4_spmd, body=%wide.region_2.3_spmd.sunk | while | flops 78872584 | bytes 9176235 | solution.py:102
  334.1 16.7 %copy.45 = f32[8,2,8192]{1,0,2:T(8,128)} copy(f32[8,2,8192]{2,1,0:T(2,128)} %get-tuple-element.194) | data formatting | bytes 1048576
  350.8 21.4 %reshape.61 = f32[8192,16]{1,0:T(8,128)} reshape(f32[8192,8,2]{2,1,0:T(8,128)} %bitcast.168) | data formatting | bytes 1048576
  372.2 144.2 %reduce-scatter.4.cloned.1.call-done = f32[128,16]{1,0:T(8,128)} async-done(((f32[8192,16]{1,0:T(8,128)}), f32[128,16]{1,0:T(8,128)}) %reduce-scatter.4.cloned.1.call-update) | async-done | bytes 8208
  516.4 1.0 reshape.62
  (134 shorter events, 68.3 us)
Async XLA Ops:
  6.5 133.2 %all-gather.3.cloned.1.call-start = ((), (), s32[]{:S(2)}) async-start(), calls=%async_computation.1 | async-start | bytes 4202496 | tf_op jit(solution)/shard_map/all_gather | solution.py:120
  7.7 83.2 %collective-permute-start.1 = (bf16[2,3,8,8192]{3,2,0,1:T(8,128)(2,1)S(1)}, bf16[2,3,8,8192]{3,2,0,1:T(8,128)(2,1)S(1)}, u32[]{:S(2)}, u32[]{:S(2)}) collective-permute-start(bf16[2,3,8,8192]{3,2,0,1:T(8,128)(2,1)S(1)} %copy.17), channel_id=1, source_target_pairs={{8,0},{16,8},{24,16},{32,24},{40,32},{48,40},{56,48},{64,56},{72,6... | collective-permute-start | bytes 2359304 | tf_op jit(solution)/shard_map/ppermute | solution.py:17
  16.5 75.3 %collective-permute-start = (bf16[2,3,8,8192]{3,2,0,1:T(8,128)(2,1)S(1)}, bf16[2,3,8,8192]{3,2,0,1:T(8,128)(2,1)}, u32[]{:S(2)}, u32[]{:S(2)}) collective-permute-start(bf16[2,3,8,8192]{3,2,0,1:T(8,128)(2,1)S(1)} %copy.17), channel_id=1, source_target_pairs={{0,8},{8,16},{16,24},{24,32},{32,40},{40,48},{48,56},{56,64},{64,7... | collective-permute-start | bytes 2359304 | tf_op jit(solution)/shard_map/ppermute | solution.py:14
  18.5 497.9 %reduce-scatter.4.cloned.1.call-start = ((), (), s32[]{:S(2)}) async-start(), calls=%async_computation.2 | async-start | bytes 4259840
  89.1 2.6 copy-start
  90.9 0.9 copy-start.1
Sparse Core Ops, SparseCore 0:
  18.6 121.1 all-gather.2
  372.3 143.9 reduce-scatter.3
where the time goes:
time: 533 us; the launch traced here: 525 us
  waiting for transfers between devices  191 us (36%)
  matrix products  115 us (22%)
  local copies, waits for them, and re-layouts  104 us (20%)
  blocking collectives  64.8 us (12%)
  other arithmetic  26.3 us (5%)
  between operations  13.5 us (3%)
  starting transfers between devices  10.8 us (2%)
    unnamed x3, waiting for transfers between devices  144 us
    dot_general x32, matrix products, add_block(): jnp.dot(rows_part.T, outer, precision=lax.Precision.HIGHEST, preferred_el...  112 us
    all_gather x1, blocking collectives, local(): lax.all_gather(packed, ('elec', 'cell'), axis=0, tiled=True)  64.8 us
    all_gather x1, waiting for transfers between devices, local(): lax.all_gather(values, ('elec', 'cell'), axis=0, tiled=True)  46.4 us
    unnamed x9, local copies, waits for them, and re-layouts  42 us
    dynamic_slice x32, local copies, waits for them, and re-layouts, add_block(): lax.dynamic_slice_in_dim(col_diff, number * row_step, row_step, 0)  30.3 us
    dynamic_slice x32, local copies, waits for them, and re-layouts, add_block(): lax.dynamic_slice_in_dim(values, number * row_step, row_step, 0)  29.8 us
    mul x32, other arithmetic, add_block(): values_part[:, :, None] * cols_part[:, None, :]  11.6 us
  transfers between devices with their start and end apart: 4, of which 2 were waited for; matrix products, arithmetic and copies ran while one was open for 2% of the time, Pallas kernels for 0%

commit v1 on v0

v1 whole, which is shorter than its diff:
```python
import functools

import jax
import jax.numpy as jnp
from jax import lax
from jax.experimental import pallas as pl
from jax.experimental.pallas import tpu as pltpu
from jax.sharding import PartitionSpec as P

X_CHIPS = 4
PER_GROUP = 8
FRAMES = 8
CAP = 4
SLOT = 32
WINDOW = 3 * PER_GROUP
F32 = jnp.float32
BF16 = jnp.bfloat16


def iota(shape, dim):
    return lax.broadcasted_iota(jnp.int32, shape, dim)


def split3(value):
    high = value.astype(BF16)
    rest = value - high.astype(F32)
    middle = rest.astype(BF16)
    low = (rest - middle.astype(F32)).astype(BF16)
    return high, middle, low


def dot_nt(left, right):
    return lax.dot_general(left, right, (((1,), (1,)), ((), ())), preferred_element_type=F32)


def drain(ref, sem):
    pltpu.make_async_copy(ref, ref, sem).wait()


def kernel(
    sizes,
    fields, resid_in, group_in, offs_in, bstep_in, sides_in,
    out,
    resid, group, offs, bstep, sides,
    own, low, high, mid,
    slots, a_buf, b_send, b_buf, c_send, c_buf, weights,
    part, core_recv, x_send, x_recv, z_send, z_recv,
    in_sem, own_sem, halo_send_sem, halo_recv_sem,
    stage_send_sem, stage_recv_sem,
    core_send_sem, core_recv_sem, x_send_sem, x_recv_sem, z_send_sem, z_recv_sem,
):
    nz, nx, ny = sizes
    lines = 2 * nx
    groups = nz * lines
    quads = resid.shape[1]
    elec = lax.axis_index("elec")
    cell = lax.axis_index("cell")
    z = elec // lines
    p = elec % lines
    x = p // 2
    core = p % 2

    inputs = [
        pltpu.make_async_copy(source, target, in_sem.at[number])
        for number, (source, target) in enumerate(
            zip((resid_in, group_in, offs_in, bstep_in, sides_in), (resid, group, offs, bstep, sides))
        )
    ]
    for copy in inputs:
        copy.start()

    def line_peer(d):
        return {"elec": z * lines + (p + d) % lines}

    def z_peer(d):
        return {"elec": ((z + d) % nz) * lines + p}

    def x_peer(d):
        return {"elec": z * lines + ((x + d) % nx) * 2 + core}

    def y_peer(d):
        return {"cell": (cell + d) % ny}

    core_peer = {"elec": z * lines + x * 2 + 1 - core}
    next_peer = {"elec": (elec + 1) % groups}
    prev_peer = {"elec": (elec + groups - 1) % groups}

    if groups < 64:
        b_buf[...] = jnp.zeros_like(b_buf)
    barrier = pltpu.get_barrier_semaphore()
    peers = (
        [line_peer(d) for d in range(1, lines)]
        + [z_peer(d) for d in range(1, nz)]
        + [y_peer(d) for d in range(1, ny)]
        + [next_peer, prev_peer]
    )
    for peer in peers:
        pl.semaphore_signal(barrier, inc=1, device_id=peer, device_id_type=pl.DeviceIdType.MESH)

    own_copy = pltpu.make_async_copy(fields, own, own_sem)
    own_copy.start()

    def send(source, target, send_sem, recv_sem, peer):
        pltpu.make_async_remote_copy(
            src_ref=source, dst_ref=target, send_sem=send_sem, recv_sem=recv_sem,
            device_id=peer, device_id_type=pl.DeviceIdType.MESH,
        ).start()

    def send_halo(c):
        send(fields.at[:, c], low.at[:, c], halo_send_sem.at[0], halo_recv_sem.at[0], next_peer)
        send(fields.at[:, c], high.at[:, c], halo_send_sem.at[1], halo_recv_sem.at[1], prev_peer)

    for copy in inputs:
        copy.wait()
    owner = group[...]
    source_a = offs[pl.ds(0, 1), :]
    source_b = (source_a + bstep[...]) % PER_GROUP
    group_m = jnp.clip(owner + sides[pl.ds(0, 1), :], 0, groups - 1)
    group_n = jnp.clip(owner + sides[pl.ds(1, 1), :], 0, groups - 1)
    column_m = (group_m - owner + 1) * PER_GROUP + offs[pl.ds(1, 1), :]
    column_n = (group_n - owner + 1) * PER_GROUP + offs[pl.ds(2, 1), :]
    row = iota((groups, quads), 0)
    names = (row % nz) * lines + row // nz
    member = jnp.where(names == owner, 1.0, 0.0).astype(F32)
    earlier = jnp.where(iota((quads, quads), 0) < iota((quads, quads), 1), 1.0, 0.0).astype(BF16)
    before = jnp.dot(member.astype(BF16), earlier, preferred_element_type=F32)
    rank = jnp.sum(member * before, axis=0, keepdims=True)
    place = iota((8, quads), 0)
    indices = jnp.where(
        place == 0, source_a,
        jnp.where(place == 1, source_b, jnp.where(place == 2, column_m, jnp.where(place == 3, column_n, 0))),
    ).astype(F32)
    real = -resid[pl.ds(0, FRAMES, stride=2), :]
    imag = -resid[pl.ds(1, FRAMES, stride=2), :]
    entry = jnp.concatenate([real, imag, indices, jnp.zeros_like(indices)], axis=0)
    entries = jnp.concatenate(
        [jnp.where(rank == float(k), entry, 0.0) for k in range(CAP)], axis=0
    )
    named = member.astype(BF16)
    sorted_rows = sum(dot_nt(named, piece) for piece in split3(entries)[::-1])
    for line in range(lines):
        slots[line] = sorted_rows[line * nz:(line + 1) * nz, :]

    pl.semaphore_wait(barrier, len(peers))

    for d in range(1, lines):
        send(slots.at[(p + d) % lines], a_buf.at[pl.ds((d - 1) * nz, nz)],
             stage_send_sem.at[0], stage_recv_sem.at[0], line_peer(d))
    for c in range(3):
        send_halo(c)
    a_buf[pl.ds((lines - 1) * nz, nz), :] = slots[p]
    own_copy.wait()
    for part_index in range(2):
        for c in range(3):
            mid[part_index, c] = own[part_index, c].astype(F32)
    arrived = a_buf.at[pl.ds(0, (lines - 1) * nz)]
    drain(arrived, stage_recv_sem.at[0])
    for to in range(nz):
        b_send[to] = a_buf[pl.ds(to, lines, stride=nz), :]
    for d in range(1, nz):
        send(b_send.at[(z + d) % nz], b_buf.at[pl.ds((d - 1) * lines, lines)],
             stage_send_sem.at[1], stage_recv_sem.at[1], z_peer(d))
    b_buf[pl.ds((nz - 1) * lines, lines), :] = b_send[z]
    drain(b_buf.at[pl.ds(0, (nz - 1) * lines)], stage_recv_sem.at[1])

    received = b_buf[...]
    both = jnp.concatenate([received, pltpu.roll(received, 64, 1)], axis=0)
    turned = both.T
    terms = []
    columns = []
    for half in range(2):
        block = turned[half * SLOT:(half + 1) * SLOT, :]
        at_a = block[16:17].astype(jnp.int32)
        at_b = block[17:18].astype(jnp.int32)
        at_m = block[18:19].astype(jnp.int32)
        at_n = block[19:20].astype(jnp.int32)
        pieces = []
        for o in range(2):
            values = block[o * 8:(o + 1) * 8]
            for e in range(PER_GROUP):
                sign = jnp.where(at_a == e, 1.0, 0.0) - jnp.where(at_b == e, 1.0, 0.0)
                pieces.append(values * sign)
        terms.append(jnp.concatenate(pieces, axis=0))
        place = iota((WINDOW, 128), 0)
        columns.append((jnp.where(place == at_m, 1.0, 0.0) - jnp.where(place == at_n, 1.0, 0.0)).astype(BF16))
    band = jnp.zeros((WINDOW, 128), F32)
    for half in range(2):
        for piece in split3(terms[half])[::-1]:
            band = band + dot_nt(columns[half], piece)
    c_send[...] = band
    for d in range(1, ny):
        send(c_send, c_buf.at[d - 1], stage_send_sem.at[2], stage_recv_sem.at[2], y_peer(d))
    drain(c_buf, stage_recv_sem.at[2])
    for d in range(ny - 1):
        band = band + c_buf[d]
    band = band.astype(BF16).astype(F32)
    upper = jnp.concatenate([band, jnp.zeros((128 - WINDOW, 128), F32)], axis=0).T
    lower = jnp.concatenate([upper[64:], -upper[:64]], axis=0)
    first = upper + pltpu.roll(lower, WINDOW, 1)
    second = pltpu.roll(first, 2 * WINDOW, 1)
    third = pltpu.roll(first, 4 * WINDOW, 1)
    lane = iota((128, 128), 1)
    nothing = jnp.zeros((128, 128), BF16)
    weights[pl.ds(0, 128), pl.ds(0, 128)] = first.astype(BF16)
    weights[pl.ds(0, 128), pl.ds(128, 128)] = nothing
    weights[pl.ds(128, 128), pl.ds(0, 128)] = second.astype(BF16)
    weights[pl.ds(128, 128), pl.ds(128, 128)] = nothing
    weights[pl.ds(256, 128), pl.ds(0, 128)] = jnp.where(lane >= 4 * WINDOW, third, 0.0).astype(BF16)
    weights[pl.ds(256, 128), pl.ds(128, 128)] = jnp.where(lane < 2 * WINDOW, third, 0.0).astype(BF16)

    drain(low, halo_recv_sem.at[0])
    drain(high, halo_recv_sem.at[1])

    def z_step(s):
        return nz // 2 + (1 - 2 * (s % 2)) * ((s + 1) // 2)

    def compute(s):
        base = ((z + z_step(s)) % nz) * (lines * 128)
        matrix = weights[...][:, :3 * 2 * WINDOW]
        for chip in range(nx):
            lanes = pl.ds(pl.multiple_of(base + chip * 256, 256), 256)
            total_real = jnp.zeros((FRAMES, 256), F32)
            total_imag = jnp.zeros((FRAMES, 256), F32)
            window = []
            for c in range(3):
                for i in range(2):
                    window += [low[i, c, :, lanes].astype(F32), mid[i, c, :, lanes], high[i, c, :, lanes].astype(F32)]
            window = jnp.concatenate(window, axis=0).astype(BF16)
            adjoint = jnp.dot(matrix, window, preferred_element_type=F32)
            for c in range(3):
                for e in range(PER_GROUP):
                    mid_real = mid[0, c, pl.ds(e, 1), lanes]
                    mid_imag = mid[1, c, pl.ds(e, 1), lanes]
                    at = c * 128 + e * 8
                    adj_real = adjoint[at:at + 8]
                    adj_imag = adjoint[at + 64:at + 72]
                    total_real = total_real + mid_real * adj_real + mid_imag * adj_imag
                    total_imag = total_imag + mid_real * adj_imag - mid_imag * adj_real
            for k in range(2):
                part[s, k, chip, pl.ds(0, 8), :] = total_real[:, k * 128:(k + 1) * 128]
                part[s, k, chip, pl.ds(8, 8), :] = total_imag[:, k * 128:(k + 1) * 128]
        send(part.at[s, 1 - core], core_recv.at[s], core_send_sem, core_recv_sem.at[s], core_peer)

    def add_core(s):
        drain(core_recv.at[s], core_recv_sem.at[s])
        x_send[s] = part[s, core] + core_recv[s]
        for d in range(1, nx):
            send(x_send.at[s, (x + d) % nx], x_recv.at[s, d - 1], x_send_sem, x_recv_sem.at[s], x_peer(d))

    def add_x(s):
        drain(x_recv.at[s], x_recv_sem.at[s])
        total = x_send[s, x]
        for d in range(nx - 1):
            total = total + x_recv[s, d]
        return total

    def pass_z(s):
        z_send[s] = add_x(s)
        send(z_send.at[s], z_recv.at[s], z_send_sem, z_recv_sem, z_peer(z_step(s)))

    core_lag = 2
    x_lag = 5

    def step(s, carry):
        @pl.when(s < nz)
        def _():
            compute(s)

        @pl.when((s >= core_lag) & (s < nz + core_lag))
        def _():
            add_core(s - core_lag)

        @pl.when((s >= x_lag) & (s < nz - 1 + x_lag))
        def _():
            pass_z(s - x_lag)

        return carry

    lax.fori_loop(0, nz - 1 + x_lag, step, 0)
    total = add_x(nz - 1)
    drain(z_recv, z_recv_sem)
    for s in range(nz - 1):
        total = total + z_recv[s]
    out[pl.ds(0, FRAMES, stride=2), :] = total[0:8]
    out[pl.ds(1, FRAMES, stride=2), :] = total[8:16]

    drain(low, halo_send_sem.at[0])
    drain(high, halo_send_sem.at[1])
    drain(arrived, stage_send_sem.at[0])
    drain(b_buf.at[pl.ds(0, (nz - 1) * lines)], stage_send_sem.at[1])
    drain(c_buf, stage_send_sem.at[2])
    drain(core_recv, core_send_sem)
    drain(x_recv, x_send_sem)
    drain(z_recv, z_send_sem)


def local(fields, residual, quad_group, offsets, b_step, sides):
    groups = lax.axis_size("elec")
    ny = lax.axis_size("cell")
    nx = X_CHIPS
    lines = 2 * nx
    nz = groups // lines
    cells = fields.shape[3]
    count = residual.shape[0]
    resid = jnp.transpose(residual, (1, 2, 0)).reshape(2 * FRAMES, count)
    vmem = pl.BlockSpec(memory_space=pltpu.VMEM)
    field_shape = (2, 3, PER_GROUP, cells)
    dma = pltpu.SemaphoreType.DMA
    gradient = pl.pallas_call(
        functools.partial(kernel, (nz, nx, ny)),
        out_shape=jax.ShapeDtypeStruct((2 * FRAMES, 128), F32),
        in_specs=[pl.BlockSpec(memory_space=pltpu.HBM)] * 6,
        out_specs=vmem,
        scratch_shapes=[
            pltpu.VMEM((2 * FRAMES, count), F32),
            pltpu.VMEM((1, count), jnp.int32),
            pltpu.VMEM((3, count), jnp.int32),
            pltpu.VMEM((1, count), jnp.int32),
            pltpu.VMEM((2, count), jnp.int32),
            pltpu.VMEM(field_shape, BF16),
            pltpu.VMEM(field_shape, BF16),
            pltpu.VMEM(field_shape, BF16),
            pltpu.VMEM(field_shape, F32),
            pltpu.VMEM((lines, nz, 128), F32),
            pltpu.VMEM((groups, 128), F32),
            pltpu.VMEM((nz, lines, 128), F32),
            pltpu.VMEM((64, 128), F32),
            pltpu.VMEM((WINDOW, 128), F32),
            pltpu.VMEM((ny - 1, WINDOW, 128), F32),
            pltpu.VMEM((384, 256), BF16),
            pltpu.VMEM((nz, 2, nx, 16, 128), F32),
            pltpu.VMEM((nz, nx, 16, 128), F32),
            pltpu.VMEM((nz, nx, 16, 128), F32),
            pltpu.VMEM((nz, nx - 1, 16, 128), F32),
            pltpu.VMEM((nz, 16, 128), F32),
            pltpu.VMEM((nz - 1, 16, 128), F32),
            dma((5,)), dma, dma((2,)), dma((2,)),
            dma((3,)), dma((3,)),
            dma, dma((nz,)), dma, dma((nz,)), dma, dma,
        ],
        compiler_params=pltpu.CompilerParams(
            collective_id=0, has_side_effects=True, vmem_limit_bytes=63 * 1024 * 1024
        ),
    )(fields, resid, quad_group.T, offsets.T, b_step.T, sides.T)
    return gradient.reshape(FRAMES, 2, 1, 128)


def solution(mesh):
    return jax.shard_map(
        local,
        mesh=mesh,
        in_specs=(
            P(None, None, "elec", "cell"),
            P(("elec", "cell"), None, None),
            P(("elec", "cell"), None),
            P(("elec", "cell"), None),
            P(("elec", "cell"), None),
            P(("elec", "cell"), None),
        ),
        out_specs=P(None, None, "cell", "elec"),
        check_vma=False,
    )
```

time: 533 us -> 48 us (0.09); the launches traced: 525 us -> 47.8 us
  waiting for transfers between devices: 191 us -> 0 us
  matrix products: 115 us -> 0 us
  local copies, waits for them, and re-layouts: 104 us -> 1.3 us
  blocking collectives: 64.8 us -> 0 us
  Pallas kernels: 0 us -> 46.4 us
  other arithmetic: 26.3 us -> 0 us
  between operations: 13.5 us -> 0.01 us
  starting transfers between devices: 10.8 us -> 0 us
    unnamed x3 -> x0, waiting for transfers between devices: 144 us -> none
    dot_general x36 -> x0, matrix products: 115 us -> none  [the longest x32 112 us: add_block(): jnp.dot(rows_part.T, outer, precision=lax.Precision.HIGHEST, preferred_el...]
    all_gather x1 -> x0, blocking collectives: 64.8 us -> none  [local(): lax.all_gather(packed, ('elec', 'cell'), axis=0, tiled=True)]
    dynamic_slice x64 -> x0, local copies, waits for them, and re-layouts: 60.1 us -> none  [the longest x32 30.3 us: add_block(): lax.dynamic_slice_in_dim(col_diff, number * row_step, row_step, 0)]
    pallas_call x0 -> x1, Pallas kernels: none -> 46.4 us  [local(): pl.pallas_call(functools.partial(kernel, (nz, nx, ny)), out_shape=jax.Sha...]
    all_gather x1 -> x0, waiting for transfers between devices: 46.4 us -> none  [local(): lax.all_gather(values, ('elec', 'cell'), axis=0, tiled=True)]
    unnamed x9 -> x1, local copies, waits for them, and re-layouts: 42 us -> 1.3 us
    mul x33 -> x0, other arithmetic: 13.3 us -> none  [the longest x32 11.6 us: add_block(): values_part[:, :, None] * cols_part[:, None, :]]
  transfers between devices with their start and end apart: 4 -> 0, of which waited for: 2 -> 0; matrix products, arithmetic and copies ran while one was open for 2% -> 0% of each run, Pallas kernels for 0% -> 0%
where the time goes in v1:
time: 48 us; the launch traced here: 47.8 us
  Pallas kernels  46.4 us (97%)
  local copies, waits for them, and re-layouts  1.3 us (3%)
    pallas_call x1, Pallas kernels, local(): pl.pallas_call(functools.partial(kernel, (nz, nx, ny)), out_shape=jax.Sha...  46.4 us
    unnamed x1, local copies, waits for them, and re-layouts  1.3 us

profile of v1, /device:TPU:1, one launch (start us, length us, event | category | flops | bytes accessed | tf_op | source)
XLA Modules:
  0.0 47.8 jit_solution(7958044450443094149)
XLA Ops:
  0.0 46.4 %shard_map.64 = f32[16,128]{1,0:T(8,128)} custom-call(bf16[2,3,8,8192]{3,2,1,0:T(8,128)(2,1)} %fields.1, f32[16,128]{1,0:T(8,128)} %bitcast.11, s32[1,128]{1,0:T(1,128)} %bitcast.14, s32[3,128]{1,0:T(4,128)} %bitcast.12, s32[1,128]{1,0:T(1,128)} %bitcast.15, s32[2,128]{1,0:T(2,128)} %bitcast.13), custom_call_target="tpu_custom_call" | custom-call | tf_op jit(solution)/shard_map/pallas_call | solution.py:309
  46.5 1.3 %copy.9 = f32[8,2,1,128]{3,2,1,0:T(1,128)} copy(f32[8,2,1,128]{3,2,1,0:T(1,128)} %bitcast.10) | data formatting | bytes 16384

commit v2 on v1

--- a/solution.py
+++ b/solution.py
@@ -53,6 +53,7 @@
     lines = 2 * nx
     groups = nz * lines
     quads = resid.shape[1]
+    halo_ends = (nz // 4, nz // 2)
     elec = lax.axis_index("elec")
     cell = lax.axis_index("cell")
     z = elec // lines
@@ -106,9 +107,19 @@
             device_id=peer, device_id_type=pl.DeviceIdType.MESH,
         ).start()
 
-    def send_halo(c):
-        send(fields.at[:, c], low.at[:, c], halo_send_sem.at[0], halo_recv_sem.at[0], next_peer)
-        send(fields.at[:, c], high.at[:, c], halo_send_sem.at[1], halo_recv_sem.at[1], prev_peer)
+    def z_step(s):
+        return nz // 2 + (1 - 2 * (s % 2)) * ((s + 1) // 2)
+
+    chunk = lines * 128
+
+    def chunk_lanes(row, s):
+        return pl.ds(pl.multiple_of(((row + z_step(s)) % nz) * chunk, chunk), chunk)
+
+    def send_halo(s):
+        for way, (peer, target, turn) in enumerate(((next_peer, low, 1), (prev_peer, high, groups - 1))):
+            lanes = chunk_lanes((elec + turn) % groups // lines, s)
+            send(fields.at[:, :, :, lanes], target.at[:, :, :, lanes],
+                 halo_send_sem.at[way], halo_recv_sem.at[way, s], peer)
 
     for copy in inputs:
         copy.wait()
@@ -146,8 +157,8 @@
     for d in range(1, lines):
         send(slots.at[(p + d) % lines], a_buf.at[pl.ds((d - 1) * nz, nz)],
              stage_send_sem.at[0], stage_recv_sem.at[0], line_peer(d))
-    for c in range(3):
-        send_halo(c)
+    for s in range(0, halo_ends[0]):
+        send_halo(s)
     a_buf[pl.ds((lines - 1) * nz, nz), :] = slots[p]
     own_copy.wait()
     for part_index in range(2):
@@ -160,6 +171,8 @@
     for d in range(1, nz):
         send(b_send.at[(z + d) % nz], b_buf.at[pl.ds((d - 1) * lines, lines)],
              stage_send_sem.at[1], stage_recv_sem.at[1], z_peer(d))
+    for s in range(halo_ends[0], halo_ends[1]):
+        send_halo(s)
     b_buf[pl.ds((nz - 1) * lines, lines), :] = b_send[z]
     drain(b_buf.at[pl.ds(0, (nz - 1) * lines)], stage_recv_sem.at[1])
 
@@ -190,6 +203,8 @@
     c_send[...] = band
     for d in range(1, ny):
         send(c_send, c_buf.at[d - 1], stage_send_sem.at[2], stage_recv_sem.at[2], y_peer(d))
+    for s in range(halo_ends[1], nz):
+        send_halo(s)
     drain(c_buf, stage_recv_sem.at[2])
     for d in range(ny - 1):
         band = band + c_buf[d]
@@ -208,14 +223,11 @@
     weights[pl.ds(256, 128), pl.ds(0, 128)] = jnp.where(lane >= 4 * WINDOW, third, 0.0).astype(BF16)
     weights[pl.ds(256, 128), pl.ds(128, 128)] = jnp.where(lane < 2 * WINDOW, third, 0.0).astype(BF16)
 
-    drain(low, halo_recv_sem.at[0])
-    drain(high, halo_recv_sem.at[1])
-
-    def z_step(s):
-        return nz // 2 + (1 - 2 * (s % 2)) * ((s + 1) // 2)
-
     def compute(s):
-        base = ((z + z_step(s)) % nz) * (lines * 128)
+        base = ((z + z_step(s)) % nz) * chunk
+        lanes = chunk_lanes(z, s)
+        drain(low.at[:, :, :, lanes], halo_recv_sem.at[0, s])
+        drain(high.at[:, :, :, lanes], halo_recv_sem.at[1, s])
         matrix = weights[...][:, :3 * 2 * WINDOW]
         for chip in range(nx):
             lanes = pl.ds(pl.multiple_of(base + chip * 256, 256), 256)
@@ -334,7 +346,7 @@
             pltpu.VMEM((nz, nx - 1, 16, 128), F32),
             pltpu.VMEM((nz, 16, 128), F32),
             pltpu.VMEM((nz - 1, 16, 128), F32),
-            dma((5,)), dma, dma((2,)), dma((2,)),
+            dma((5,)), dma, dma((2,)), dma((2, nz)),
             dma((3,)), dma((3,)),
             dma, dma((nz,)), dma, dma((nz,)), dma, dma,
         ],

time: 48 us -> 44.3 us (0.923)
  Pallas kernels: 46.4 us -> 42.8 us
    pallas_call x1, Pallas kernels: 46.4 us -> 42.8 us  [local(): pl.pallas_call(functools.partial(kernel, (nz, nx, ny)), out_shape=jax.Sha...]
where the time goes in v2:
time: 44.3 us; the launch traced here: 44.1 us
  Pallas kernels  42.8 us (97%)
  local copies, waits for them, and re-layouts  1.3 us (3%)
    pallas_call x1, Pallas kernels, local(): pl.pallas_call(functools.partial(kernel, (nz, nx, ny)), out_shape=jax.Sha...  42.8 us
    unnamed x1, local copies, waits for them, and re-layouts  1.3 us

profile of v2, /device:TPU:1, one launch (start us, length us, event | category | flops | bytes accessed | tf_op | source)
XLA Modules:
  0.0 44.1 jit_solution(12215580311648766553)
XLA Ops:
  0.0 42.8 %shard_map.64 = f32[16,128]{1,0:T(8,128)} custom-call(bf16[2,3,8,8192]{3,2,1,0:T(8,128)(2,1)} %fields.1, f32[16,128]{1,0:T(8,128)} %bitcast.11, s32[1,128]{1,0:T(1,128)} %bitcast.14, s32[3,128]{1,0:T(4,128)} %bitcast.12, s32[1,128]{1,0:T(1,128)} %bitcast.15, s32[2,128]{1,0:T(2,128)} %bitcast.13), custom_call_target="tpu_custom_call" | custom-call | tf_op jit(solution)/shard_map/pallas_call | solution.py:321
  42.8 1.3 %copy.9 = f32[8,2,1,128]{3,2,1,0:T(1,128)} copy(f32[8,2,1,128]{3,2,1,0:T(1,128)} %bitcast.10) | data formatting | bytes 16384

commit v3 on v2

--- a/solution.py
+++ b/solution.py
@@ -42,12 +42,12 @@
     fields, resid_in, group_in, offs_in, bstep_in, sides_in,
     out,
     resid, group, offs, bstep, sides,
-    own, low, high, mid,
+    own, low, high,
     slots, a_buf, b_send, b_buf, c_send, c_buf, weights,
-    part, core_recv, x_send, x_recv, z_send, z_recv,
+    part, core_recv, sums, shares,
     in_sem, own_sem, halo_send_sem, halo_recv_sem,
     stage_send_sem, stage_recv_sem,
-    core_send_sem, core_recv_sem, x_send_sem, x_recv_sem, z_send_sem, z_recv_sem,
+    core_send_sem, core_recv_sem, share_send_sem, share_recv_sem,
 ):
     nz, nx, ny = sizes
     lines = 2 * nx
@@ -76,8 +76,8 @@
     def z_peer(d):
         return {"elec": ((z + d) % nz) * lines + p}
 
-    def x_peer(d):
-        return {"elec": z * lines + ((x + d) % nx) * 2 + core}
+    def chip_peer(dz, dx):
+        return {"elec": ((z + dz) % nz) * lines + ((x + dx) % nx) * 2 + core}
 
     def y_peer(d):
         return {"cell": (cell + d) % ny}
@@ -91,7 +91,7 @@
     barrier = pltpu.get_barrier_semaphore()
     peers = (
         [line_peer(d) for d in range(1, lines)]
-        + [z_peer(d) for d in range(1, nz)]
+        + [chip_peer(dz, dx) for dz in range(1, nz) for dx in range(nx)]
         + [y_peer(d) for d in range(1, ny)]
         + [next_peer, prev_peer]
     )
@@ -161,9 +161,6 @@
         send_halo(s)
     a_buf[pl.ds((lines - 1) * nz, nz), :] = slots[p]
     own_copy.wait()
-    for part_index in range(2):
-        for c in range(3):
-            mid[part_index, c] = own[part_index, c].astype(F32)
     arrived = a_buf.at[pl.ds(0, (lines - 1) * nz)]
     drain(arrived, stage_recv_sem.at[0])
     for to in range(nz):
@@ -187,13 +184,9 @@
         at_b = block[17:18].astype(jnp.int32)
         at_m = block[18:19].astype(jnp.int32)
         at_n = block[19:20].astype(jnp.int32)
-        pieces = []
-        for o in range(2):
-            values = block[o * 8:(o + 1) * 8]
-            for e in range(PER_GROUP):
-                sign = jnp.where(at_a == e, 1.0, 0.0) - jnp.where(at_b == e, 1.0, 0.0)
-                pieces.append(values * sign)
-        terms.append(jnp.concatenate(pieces, axis=0))
+        place = iota((PER_GROUP, 128), 0)
+        sign = jnp.where(place == at_a, 1.0, 0.0) - jnp.where(place == at_b, 1.0, 0.0)
+        terms.append(jnp.concatenate([block[k:k + 1] * sign for k in range(2 * FRAMES)], axis=0))
         place = iota((WINDOW, 128), 0)
         columns.append((jnp.where(place == at_m, 1.0, 0.0) - jnp.where(place == at_n, 1.0, 0.0)).astype(BF16))
     band = jnp.zeros((WINDOW, 128), F32)
@@ -223,76 +216,89 @@
     weights[pl.ds(256, 128), pl.ds(0, 128)] = jnp.where(lane >= 4 * WINDOW, third, 0.0).astype(BF16)
     weights[pl.ds(256, 128), pl.ds(128, 128)] = jnp.where(lane < 2 * WINDOW, third, 0.0).astype(BF16)
 
+    sublane = iota((PER_GROUP, 128), 0)
+
+    def fold(first, second, width):
+        keep = sublane % (2 * width) < width
+        return jnp.where(keep, first, second) + pltpu.roll(
+            jnp.where(keep, second, first), PER_GROUP - width, 0
+        )
+
+    def collect(rows):
+        for width in (1, 2, 4):
+            rows = [fold(rows[k], rows[k + 1], width) for k in range(0, len(rows), 2)]
+        return rows[0]
+
     def compute(s):
         base = ((z + z_step(s)) % nz) * chunk
-        lanes = chunk_lanes(z, s)
-        drain(low.at[:, :, :, lanes], halo_recv_sem.at[0, s])
-        drain(high.at[:, :, :, lanes], halo_recv_sem.at[1, s])
+        arrived_lanes = chunk_lanes(z, s)
+        drain(low.at[:, :, :, arrived_lanes], halo_recv_sem.at[0, s])
+        drain(high.at[:, :, :, arrived_lanes], halo_recv_sem.at[1, s])
         matrix = weights[...][:, :3 * 2 * WINDOW]
         for chip in range(nx):
             lanes = pl.ds(pl.multiple_of(base + chip * 256, 256), 256)
-            total_real = jnp.zeros((FRAMES, 256), F32)
-            total_imag = jnp.zeros((FRAMES, 256), F32)
+            middle = [[own[i, c, :, lanes].astype(F32) for i in range(2)] for c in range(3)]
             window = []
             for c in range(3):
                 for i in range(2):
-                    window += [low[i, c, :, lanes].astype(F32), mid[i, c, :, lanes], high[i, c, :, lanes].astype(F32)]
+                    window += [low[i, c, :, lanes].astype(F32), middle[c][i], high[i, c, :, lanes].astype(F32)]
             window = jnp.concatenate(window, axis=0).astype(BF16)
             adjoint = jnp.dot(matrix, window, preferred_element_type=F32)
-            for c in range(3):
-                for e in range(PER_GROUP):
-                    mid_real = mid[0, c, pl.ds(e, 1), lanes]
-                    mid_imag = mid[1, c, pl.ds(e, 1), lanes]
-                    at = c * 128 + e * 8
-                    adj_real = adjoint[at:at + 8]
-                    adj_imag = adjoint[at + 64:at + 72]
-                    total_real = total_real + mid_real * adj_real + mid_imag * adj_imag
-                    total_imag = total_imag + mid_real * adj_imag - mid_imag * adj_real
             for k in range(2):
-                part[s, k, chip, pl.ds(0, 8), :] = total_real[:, k * 128:(k + 1) * 128]
-                part[s, k, chip, pl.ds(8, 8), :] = total_imag[:, k * 128:(k + 1) * 128]
+                half = slice(k * 128, (k + 1) * 128)
+                real = []
+                imag = []
+                for t in range(FRAMES):
+                    total_real = jnp.zeros((PER_GROUP, 128), F32)
+                    total_imag = jnp.zeros((PER_GROUP, 128), F32)
+                    for c in range(3):
+                        at = c * 128 + t * 8
+                        adj_real = adjoint[at:at + 8, half]
+                        adj_imag = adjoint[at + 64:at + 72, half]
+                        mid_real = middle[c][0][:, half]
+                        mid_imag = middle[c][1][:, half]
+                        total_real = total_real + mid_real * adj_real + mid_imag * adj_imag
+                        total_imag = total_imag + mid_real * adj_imag - mid_imag * adj_real
+                    real.append(total_real)
+                    imag.append(total_imag)
+                part[s, k, chip, pl.ds(0, 8), :] = collect(real)
+                part[s, k, chip, pl.ds(8, 8), :] = collect(imag)
         send(part.at[s, 1 - core], core_recv.at[s], core_send_sem, core_recv_sem.at[s], core_peer)
+
+    def share(s, d):
+        send(sums.at[s, (x + d) % nx], shares.at[s * nx + (d + nx - 1) % nx],
+             share_send_sem, share_recv_sem.at[s], chip_peer(z_step(s), d))
 
     def add_core(s):
         drain(core_recv.at[s], core_recv_sem.at[s])
-        x_send[s] = part[s, core] + core_recv[s]
+        sums[s] = part[s, core] + core_recv[s]
         for d in range(1, nx):
-            send(x_send.at[s, (x + d) % nx], x_recv.at[s, d - 1], x_send_sem, x_recv_sem.at[s], x_peer(d))
-
-    def add_x(s):
-        drain(x_recv.at[s], x_recv_sem.at[s])
-        total = x_send[s, x]
-        for d in range(nx - 1):
-            total = total + x_recv[s, d]
-        return total
-
-    def pass_z(s):
-        z_send[s] = add_x(s)
-        send(z_send.at[s], z_recv.at[s], z_send_sem, z_recv_sem, z_peer(z_step(s)))
+            share(s, d)
+
+        @pl.when(s < nz - 1)
+        def _():
+            share(s, 0)
 
     core_lag = 2
-    x_lag = 5
 
     def step(s, carry):
         @pl.when(s < nz)
         def _():
             compute(s)
 
-        @pl.when((s >= core_lag) & (s < nz + core_lag))
+        @pl.when(s >= core_lag)
         def _():
             add_core(s - core_lag)
 
-        @pl.when((s >= x_lag) & (s < nz - 1 + x_lag))
-        def _():
-            pass_z(s - x_lag)
-
         return carry
 
-    lax.fori_loop(0, nz - 1 + x_lag, step, 0)
-    total = add_x(nz - 1)
-    drain(z_recv, z_recv_sem)
-    for s in range(nz - 1):
-        total = total + z_recv[s]
+    lax.fori_loop(0, nz + core_lag, step, 0)
+    total = sums[nz - 1, x]
+    for s in range(nz):
+        count = nx if s < nz - 1 else nx - 1
+        drain(shares.at[pl.ds(s * nx, count)], share_recv_sem.at[s])
+        for d in range(count):
+            total = total + shares[s * nx + d]
     out[pl.ds(0, FRAMES, stride=2), :] = total[0:8]
     out[pl.ds(1, FRAMES, stride=2), :] = total[8:16]
 
@@ -302,8 +308,7 @@
     drain(b_buf.at[pl.ds(0, (nz - 1) * lines)], stage_send_sem.at[1])
     drain(c_buf, stage_send_sem.at[2])
     drain(core_recv, core_send_sem)
-    drain(x_recv, x_send_sem)
-    drain(z_recv, z_send_sem)
+    drain(shares.at[pl.ds(0, nz * nx - 1)], share_send_sem)
 
 
 def local(fields, residual, quad_group, offsets, b_step, sides):
@@ -332,7 +337,6 @@
             pltpu.VMEM(field_shape, BF16),
             pltpu.VMEM(field_shape, BF16),
             pltpu.VMEM(field_shape, BF16),
-            pltpu.VMEM(field_shape, F32),
             pltpu.VMEM((lines, nz, 128), F32),
             pltpu.VMEM((groups, 128), F32),
             pltpu.VMEM((nz, lines, 128), F32),
@@ -343,17 +347,18 @@
             pltpu.VMEM((nz, 2, nx, 16, 128), F32),
             pltpu.VMEM((nz, nx, 16, 128), F32),
             pltpu.VMEM((nz, nx, 16, 128), F32),
-            pltpu.VMEM((nz, nx - 1, 16, 128), F32),
-            pltpu.VMEM((nz, 16, 128), F32),
-            pltpu.VMEM((nz - 1, 16, 128), F32),
+            pltpu.VMEM((nz * nx, 16, 128), F32),
             dma((5,)), dma, dma((2,)), dma((2, nz)),
             dma((3,)), dma((3,)),
-            dma, dma((nz,)), dma, dma((nz,)), dma, dma,
+            dma, dma((nz,)), dma, dma((nz,)),
         ],
         compiler_params=pltpu.CompilerParams(
-            collective_id=0, has_side_effects=True, vmem_limit_bytes=63 * 1024 * 1024
+            collective_id=0, has_side_effects=True, vmem_limit_bytes=40 * 1024 * 1024
         ),
-    )(fields, resid, quad_group.T, offsets.T, b_step.T, sides.T)
+    )(*(
+        pltpu.with_memory_space_constraint(value, pltpu.HBM)
+        for value in (fields, resid, quad_group.T, offsets.T, b_step.T, sides.T)
+    ))
     return gradient.reshape(FRAMES, 2, 1, 128)
 
 

time: 44.3 us -> 43.9 us (level)
  local copies, waits for them, and re-layouts: 1.3 us -> 0.6 us
    unnamed x1, local copies, waits for them, and re-layouts: 1.3 us -> 0.6 us
where the time goes in v3:
time: 43.9 us; the launch traced here: 43.7 us
  Pallas kernels  43.1 us (98%)
  local copies, waits for them, and re-layouts  0.6 us (1%)
    pallas_call x1, Pallas kernels, local(): pl.pallas_call(functools.partial(kernel, (nz, nx, ny)), out_shape=jax.Sha...  43.1 us

profile of v3, /device:TPU:1, one launch (start us, length us, event | category | flops | bytes accessed | tf_op | source)
XLA Modules:
  0.0 43.7 jit_solution(5942079942656978877)
XLA Ops:
  0.0 43.1 %shard_map.64 = f32[16,128]{1,0:T(8,128)S(1)} custom-call(bf16[2,3,8,8192]{3,2,1,0:T(8,128)(2,1)} %fields.1, f32[16,128]{1,0:T(8,128)} %bitcast.11, s32[1,128]{1,0:T(1,128)} %bitcast.14, s32[3,128]{1,0:T(4,128)} %bitcast.12, s32[1,128]{1,0:T(1,128)} %bitcast.15, s32[2,128]{1,0:T(2,128)} %bitcast.13), custom_call_target="tpu_custom_call" | custom-call | tf_op jit(solution)/shard_map/pallas_call | solution.py:326
  43.1 0.6 %copy.9 = f32[8,2,1,128]{3,2,1,0:T(1,128)} copy(f32[8,2,1,128]{3,2,1,0:T(1,128)S(1)} %bitcast.10) | data formatting | bytes 16384

commit v4 on v3

--- a/solution.py
+++ b/solution.py
@@ -44,7 +44,7 @@
     resid, group, offs, bstep, sides,
     own, low, high,
     slots, a_buf, b_send, b_buf, c_send, c_buf, weights,
-    part, core_recv, sums, shares,
+    part, core_recv, sums, rounded, shares,
     in_sem, own_sem, halo_send_sem, halo_recv_sem,
     stage_send_sem, stage_recv_sem,
     core_send_sem, core_recv_sem, share_send_sem, share_recv_sem,
@@ -53,7 +53,7 @@
     lines = 2 * nx
     groups = nz * lines
     quads = resid.shape[1]
-    halo_ends = (nz // 4, nz // 2)
+    halo_ends = (0, 3 * nz // 8)
     elec = lax.axis_index("elec")
     cell = lax.axis_index("cell")
     z = elec // lines
@@ -266,12 +266,14 @@
         send(part.at[s, 1 - core], core_recv.at[s], core_send_sem, core_recv_sem.at[s], core_peer)
 
     def share(s, d):
-        send(sums.at[s, (x + d) % nx], shares.at[s * nx + (d + nx - 1) % nx],
+        send(rounded.at[s, (x + d) % nx], shares.at[s * nx + (d + nx - 1) % nx],
              share_send_sem, share_recv_sem.at[s], chip_peer(z_step(s), d))
 
     def add_core(s):
         drain(core_recv.at[s], core_recv_sem.at[s])
-        sums[s] = part[s, core] + core_recv[s]
+        both_cores = part[s, core] + core_recv[s]
+        sums[s] = both_cores
+        rounded[s] = both_cores.astype(BF16)
         for d in range(1, nx):
             share(s, d)
 
@@ -298,7 +300,7 @@
         count = nx if s < nz - 1 else nx - 1
         drain(shares.at[pl.ds(s * nx, count)], share_recv_sem.at[s])
         for d in range(count):
-            total = total + shares[s * nx + d]
+            total = total + shares[s * nx + d].astype(F32)
     out[pl.ds(0, FRAMES, stride=2), :] = total[0:8]
     out[pl.ds(1, FRAMES, stride=2), :] = total[8:16]
 
@@ -347,7 +349,8 @@
             pltpu.VMEM((nz, 2, nx, 16, 128), F32),
             pltpu.VMEM((nz, nx, 16, 128), F32),
             pltpu.VMEM((nz, nx, 16, 128), F32),
-            pltpu.VMEM((nz * nx, 16, 128), F32),
+            pltpu.VMEM((nz, nx, 16, 128), BF16),
+            pltpu.VMEM((nz * nx, 16, 128), BF16),
             dma((5,)), dma, dma((2,)), dma((2, nz)),
             dma((3,)), dma((3,)),
             dma, dma((nz,)), dma, dma((nz,)),

time: 43.9 us -> 41.5 us (0.945)
  Pallas kernels: 43.1 us -> 40.7 us
    pallas_call x1, Pallas kernels: 43.1 us -> 40.7 us  [local(): pl.pallas_call(functools.partial(kernel, (nz, nx, ny)), out_shape=jax.Sha...]
where the time goes in v4:
time: 41.5 us; the launch traced here: 41.4 us
  Pallas kernels  40.7 us (98%)
  local copies, waits for them, and re-layouts  0.6 us (1%)
    pallas_call x1, Pallas kernels, local(): pl.pallas_call(functools.partial(kernel, (nz, nx, ny)), out_shape=jax.Sha...  40.7 us

profile of v4, /device:TPU:1, one launch (start us, length us, event | category | flops | bytes accessed | tf_op | source)
XLA Modules:
  0.0 41.4 jit_solution(4654700779086239225)
XLA Ops:
  0.0 40.7 %shard_map.64 = f32[16,128]{1,0:T(8,128)S(1)} custom-call(bf16[2,3,8,8192]{3,2,1,0:T(8,128)(2,1)} %fields.1, f32[16,128]{1,0:T(8,128)} %bitcast.11, s32[1,128]{1,0:T(1,128)} %bitcast.14, s32[3,128]{1,0:T(4,128)} %bitcast.12, s32[1,128]{1,0:T(1,128)} %bitcast.15, s32[2,128]{1,0:T(2,128)} %bitcast.13), custom_call_target="tpu_custom_call" | custom-call | tf_op jit(solution)/shard_map/pallas_call | solution.py:328
  40.8 0.6 %copy.9 = f32[8,2,1,128]{3,2,1,0:T(1,128)} copy(f32[8,2,1,128]{3,2,1,0:T(1,128)S(1)} %bitcast.10) | data formatting | bytes 16384

commit v5 on v3

--- a/solution.py
+++ b/solution.py
@@ -44,16 +44,16 @@
     resid, group, offs, bstep, sides,
     own, low, high,
     slots, a_buf, b_send, b_buf, c_send, c_buf, weights,
-    part, core_recv, sums, shares,
+    part, core_recv, rounded, shares, near, near_shares,
     in_sem, own_sem, halo_send_sem, halo_recv_sem,
     stage_send_sem, stage_recv_sem,
-    core_send_sem, core_recv_sem, share_send_sem, share_recv_sem,
+    core_send_sem, core_recv_sem, share_send_sem, share_recv_sem, near_send_sem, near_recv_sem,
 ):
     nz, nx, ny = sizes
     lines = 2 * nx
     groups = nz * lines
     quads = resid.shape[1]
-    halo_ends = (nz // 4, nz // 2)
+    halo_ends = (0, 3 * nz // 8)
     elec = lax.axis_index("elec")
     cell = lax.axis_index("cell")
     z = elec // lines
@@ -261,30 +261,32 @@
                         total_imag = total_imag + mid_real * adj_imag - mid_imag * adj_real
                     real.append(total_real)
                     imag.append(total_imag)
-                part[s, k, chip, pl.ds(0, 8), :] = collect(real)
-                part[s, k, chip, pl.ds(8, 8), :] = collect(imag)
+                total_rows = jnp.concatenate([collect(real), collect(imag)], axis=0)
+                part[s, k, chip] = total_rows
+                near[chip * 2 + k] = total_rows.astype(BF16)
+
+    def swap_core(s):
         send(part.at[s, 1 - core], core_recv.at[s], core_send_sem, core_recv_sem.at[s], core_peer)
 
-    def share(s, d):
-        send(sums.at[s, (x + d) % nx], shares.at[s * nx + (d + nx - 1) % nx],
-             share_send_sem, share_recv_sem.at[s], chip_peer(z_step(s), d))
+    def send_near():
+        for d in range(1, lines):
+            send(near.at[(p + d) % lines], near_shares.at[d - 1], near_send_sem, near_recv_sem, line_peer(d))
 
     def add_core(s):
         drain(core_recv.at[s], core_recv_sem.at[s])
-        sums[s] = part[s, core] + core_recv[s]
-        for d in range(1, nx):
-            share(s, d)
+        rounded[s] = (part[s, core] + core_recv[s]).astype(BF16)
+        for d in range(nx):
+            send(rounded.at[s, (x + d) % nx], shares.at[s, d],
+                 share_send_sem, share_recv_sem.at[s], chip_peer(z_step(s), d))
+
+    core_lag = 2
+
+    def step(s, carry):
+        compute(s)
 
         @pl.when(s < nz - 1)
         def _():
-            share(s, 0)
-
-    core_lag = 2
-
-    def step(s, carry):
-        @pl.when(s < nz)
-        def _():
-            compute(s)
+            swap_core(s)
 
         @pl.when(s >= core_lag)
         def _():
@@ -292,13 +294,18 @@
 
         return carry
 
-    lax.fori_loop(0, nz + core_lag, step, 0)
-    total = sums[nz - 1, x]
-    for s in range(nz):
-        count = nx if s < nz - 1 else nx - 1
-        drain(shares.at[pl.ds(s * nx, count)], share_recv_sem.at[s])
-        for d in range(count):
-            total = total + shares[s * nx + d]
+    lax.fori_loop(0, nz, step, 0)
+    send_near()
+    for s in range(max(nz - core_lag, 0), nz - 1):
+        add_core(s)
+    total = part[nz - 1, core, x]
+    for s in range(nz - 1):
+        drain(shares.at[s], share_recv_sem.at[s])
+        for d in range(nx):
+            total = total + shares[s, d].astype(F32)
+    drain(near_shares, near_recv_sem)
+    for d in range(lines - 1):
+        total = total + near_shares[d].astype(F32)
     out[pl.ds(0, FRAMES, stride=2), :] = total[0:8]
     out[pl.ds(1, FRAMES, stride=2), :] = total[8:16]
 
@@ -308,7 +315,8 @@
     drain(b_buf.at[pl.ds(0, (nz - 1) * lines)], stage_send_sem.at[1])
     drain(c_buf, stage_send_sem.at[2])
     drain(core_recv, core_send_sem)
-    drain(shares.at[pl.ds(0, nz * nx - 1)], share_send_sem)
+    drain(shares, share_send_sem)
+    drain(near_shares, near_send_sem)
 
 
 def local(fields, residual, quad_group, offsets, b_step, sides):
@@ -345,12 +353,14 @@
             pltpu.VMEM((ny - 1, WINDOW, 128), F32),
             pltpu.VMEM((384, 256), BF16),
             pltpu.VMEM((nz, 2, nx, 16, 128), F32),
-            pltpu.VMEM((nz, nx, 16, 128), F32),
-            pltpu.VMEM((nz, nx, 16, 128), F32),
-            pltpu.VMEM((nz * nx, 16, 128), F32),
+            pltpu.VMEM((nz - 1, nx, 16, 128), F32),
+            pltpu.VMEM((nz - 1, nx, 16, 128), BF16),
+            pltpu.VMEM((nz - 1, nx, 16, 128), BF16),
+            pltpu.VMEM((lines, 16, 128), BF16),
+            pltpu.VMEM((lines - 1, 16, 128), BF16),
             dma((5,)), dma, dma((2,)), dma((2, nz)),
             dma((3,)), dma((3,)),
-            dma, dma((nz,)), dma, dma((nz,)),
+            dma, dma((nz - 1,)), dma, dma((nz - 1,)), dma, dma,
         ],
         compiler_params=pltpu.CompilerParams(
             collective_id=0, has_side_effects=True, vmem_limit_bytes=40 * 1024 * 1024

time: 43.9 us -> 41.6 us (0.948)
  Pallas kernels: 43.1 us -> 40.8 us
    pallas_call x1, Pallas kernels: 43.1 us -> 40.8 us  [local(): pl.pallas_call(functools.partial(kernel, (nz, nx, ny)), out_shape=jax.Sha...]
where the time goes in v5:
time: 41.6 us; the launch traced here: 41.5 us
  Pallas kernels  40.8 us (98%)
  local copies, waits for them, and re-layouts  0.6 us (1%)
    pallas_call x1, Pallas kernels, local(): pl.pallas_call(functools.partial(kernel, (nz, nx, ny)), out_shape=jax.Sha...  40.8 us

profile of v5, /device:TPU:1, one launch (start us, length us, event | category | flops | bytes accessed | tf_op | source)
XLA Modules:
  0.0 41.5 jit_solution(7711037899089615038)
XLA Ops:
  0.0 40.8 %shard_map.64 = f32[16,128]{1,0:T(8,128)S(1)} custom-call(bf16[2,3,8,8192]{3,2,1,0:T(8,128)(2,1)} %fields.1, f32[16,128]{1,0:T(8,128)} %bitcast.11, s32[1,128]{1,0:T(1,128)} %bitcast.14, s32[3,128]{1,0:T(4,128)} %bitcast.12, s32[1,128]{1,0:T(1,128)} %bitcast.15, s32[2,128]{1,0:T(2,128)} %bitcast.13), custom_call_target="tpu_custom_call" | custom-call | tf_op jit(solution)/shard_map/pallas_call | solution.py:334
  40.9 0.6 %copy.9 = f32[8,2,1,128]{3,2,1,0:T(1,128)} copy(f32[8,2,1,128]{3,2,1,0:T(1,128)S(1)} %bitcast.10) | data formatting | bytes 16384

commit v6 on v5

--- a/solution.py
+++ b/solution.py
@@ -208,13 +208,15 @@
     second = pltpu.roll(first, 2 * WINDOW, 1)
     third = pltpu.roll(first, 4 * WINDOW, 1)
     lane = iota((128, 128), 1)
-    nothing = jnp.zeros((128, 128), BF16)
-    weights[pl.ds(0, 128), pl.ds(0, 128)] = first.astype(BF16)
-    weights[pl.ds(0, 128), pl.ds(128, 128)] = nothing
-    weights[pl.ds(128, 128), pl.ds(0, 128)] = second.astype(BF16)
-    weights[pl.ds(128, 128), pl.ds(128, 128)] = nothing
-    weights[pl.ds(256, 128), pl.ds(0, 128)] = jnp.where(lane >= 4 * WINDOW, third, 0.0).astype(BF16)
-    weights[pl.ds(256, 128), pl.ds(128, 128)] = jnp.where(lane < 2 * WINDOW, third, 0.0).astype(BF16)
+    nothing = jnp.zeros((128, 128), F32)
+    left = (first, second, jnp.where(lane >= 4 * WINDOW, third, 0.0))
+    right = (nothing, nothing, jnp.where(lane < 2 * WINDOW, third, 0.0))
+    for half, blocks in enumerate((left, right)):
+        rows = [
+            blocks[c][at:at + PER_GROUP]
+            for t in range(FRAMES) for c in range(3) for at in (t * PER_GROUP, 64 + t * PER_GROUP)
+        ]
+        weights[:, pl.ds(half * 128, 128)] = jnp.concatenate(rows, axis=0).astype(BF16)
 
     sublane = iota((PER_GROUP, 128), 0)
 
@@ -252,9 +254,9 @@
                     total_real = jnp.zeros((PER_GROUP, 128), F32)
                     total_imag = jnp.zeros((PER_GROUP, 128), F32)
                     for c in range(3):
-                        at = c * 128 + t * 8
+                        at = (t * 3 + c) * 16
                         adj_real = adjoint[at:at + 8, half]
-                        adj_imag = adjoint[at + 64:at + 72, half]
+                        adj_imag = adjoint[at + 8:at + 16, half]
                         mid_real = middle[c][0][:, half]
                         mid_imag = middle[c][1][:, half]
                         total_real = total_real + mid_real * adj_real + mid_imag * adj_imag

time: 41.6 us -> 41.5 us (level)
  no operation moved by 1% of the time
where the time goes in v6:
time: 41.5 us; the launch traced here: 41.4 us
  Pallas kernels  40.7 us (98%)
  local copies, waits for them, and re-layouts  0.6 us (1%)
    pallas_call x1, Pallas kernels, local(): pl.pallas_call(functools.partial(kernel, (nz, nx, ny)), out_shape=jax.Sha...  40.7 us

profile of v6, /device:TPU:1, one launch (start us, length us, event | category | flops | bytes accessed | tf_op | source)
XLA Modules:
  0.0 41.4 jit_solution(1242764176363864609)
XLA Ops:
  0.0 40.7 %shard_map.64 = f32[16,128]{1,0:T(8,128)S(1)} custom-call(bf16[2,3,8,8192]{3,2,1,0:T(8,128)(2,1)} %fields.1, f32[16,128]{1,0:T(8,128)} %bitcast.11, s32[1,128]{1,0:T(1,128)} %bitcast.14, s32[3,128]{1,0:T(4,128)} %bitcast.12, s32[1,128]{1,0:T(1,128)} %bitcast.15, s32[2,128]{1,0:T(2,128)} %bitcast.13), custom_call_target="tpu_custom_call" | custom-call | tf_op jit(solution)/shard_map/pallas_call | solution.py:336
  40.8 0.6 %copy.9 = f32[8,2,1,128]{3,2,1,0:T(1,128)} copy(f32[8,2,1,128]{3,2,1,0:T(1,128)S(1)} %bitcast.10) | data formatting | bytes 16384

commit v7 on v6

--- a/solution.py
+++ b/solution.py
@@ -33,6 +33,10 @@
     return lax.dot_general(left, right, (((1,), (1,)), ((), ())), preferred_element_type=F32)
 
 
+def far_chunks(nz):
+    return 3 * (nz - 1) // 7
+
+
 def drain(ref, sem):
     pltpu.make_async_copy(ref, ref, sem).wait()
 
@@ -44,16 +48,18 @@
     resid, group, offs, bstep, sides,
     own, low, high,
     slots, a_buf, b_send, b_buf, c_send, c_buf, weights,
-    part, core_recv, rounded, shares, near, near_shares,
+    part, core_recv, rounded, shares, near, near_shares, row_recv, row_send, far_shares,
     in_sem, own_sem, halo_send_sem, halo_recv_sem,
     stage_send_sem, stage_recv_sem,
     core_send_sem, core_recv_sem, share_send_sem, share_recv_sem, near_send_sem, near_recv_sem,
+    row_send_sem, row_recv_sem, far_send_sem, far_recv_sem,
 ):
     nz, nx, ny = sizes
     lines = 2 * nx
     groups = nz * lines
     quads = resid.shape[1]
     halo_ends = (0, 3 * nz // 8)
+    far = far_chunks(nz)
     elec = lax.axis_index("elec")
     cell = lax.axis_index("cell")
     z = elec // lines
@@ -277,11 +283,29 @@
     def add_core(s):
         drain(core_recv.at[s], core_recv_sem.at[s])
         rounded[s] = (part[s, core] + core_recv[s]).astype(BF16)
-        for d in range(nx):
-            send(rounded.at[s, (x + d) % nx], shares.at[s, d],
-                 share_send_sem, share_recv_sem.at[s], chip_peer(z_step(s), d))
+
+        @pl.when(s < far)
+        def _():
+            for d in range(1, nx):
+                send(rounded.at[s, (x + d) % nx], row_recv.at[s, d - 1],
+                     row_send_sem, row_recv_sem.at[s], chip_peer(0, d))
+
+        @pl.when(s >= far)
+        def _():
+            for d in range(nx):
+                send(rounded.at[s, (x + d) % nx], shares.at[s - far, d],
+                     share_send_sem, share_recv_sem.at[s - far], chip_peer(z_step(s), d))
+
+    def pass_far(s):
+        drain(row_recv.at[s], row_recv_sem.at[s])
+        total = part[s, core, x] + core_recv[s, x]
+        for d in range(nx - 1):
+            total = total + row_recv[s, d].astype(F32)
+        row_send[s] = total.astype(BF16)
+        send(row_send.at[s], far_shares.at[s], far_send_sem, far_recv_sem, chip_peer(z_step(s), 0))
 
     core_lag = 2
+    row_lag = 4
 
     def step(s, carry):
         compute(s)
@@ -293,6 +317,10 @@
         @pl.when(s >= core_lag)
         def _():
             add_core(s - core_lag)
+
+        @pl.when((s >= row_lag) & (s < row_lag + far))
+        def _():
+            pass_far(s - row_lag)
 
         return carry
 
@@ -300,8 +328,13 @@
     send_near()
     for s in range(max(nz - core_lag, 0), nz - 1):
         add_core(s)
+    for s in range(max(nz - row_lag, 0), far):
+        pass_far(s)
     total = part[nz - 1, core, x]
-    for s in range(nz - 1):
+    drain(far_shares, far_recv_sem)
+    for s in range(far):
+        total = total + far_shares[s].astype(F32)
+    for s in range(nz - 1 - far):
         drain(shares.at[s], share_recv_sem.at[s])
         for d in range(nx):
             total = total + shares[s, d].astype(F32)
@@ -319,6 +352,8 @@
     drain(core_recv, core_send_sem)
     drain(shares, share_send_sem)
     drain(near_shares, near_send_sem)
+    drain(row_recv, row_send_sem)
+    drain(far_shares, far_send_sem)
 
 
 def local(fields, residual, quad_group, offsets, b_step, sides):
@@ -327,6 +362,7 @@
     nx = X_CHIPS
     lines = 2 * nx
     nz = groups // lines
+    far = far_chunks(nz)
     cells = fields.shape[3]
     count = residual.shape[0]
     resid = jnp.transpose(residual, (1, 2, 0)).reshape(2 * FRAMES, count)
@@ -357,12 +393,16 @@
             pltpu.VMEM((nz, 2, nx, 16, 128), F32),
             pltpu.VMEM((nz - 1, nx, 16, 128), F32),
             pltpu.VMEM((nz - 1, nx, 16, 128), BF16),
-            pltpu.VMEM((nz - 1, nx, 16, 128), BF16),
+            pltpu.VMEM((nz - 1 - far, nx, 16, 128), BF16),
             pltpu.VMEM((lines, 16, 128), BF16),
             pltpu.VMEM((lines - 1, 16, 128), BF16),
+            pltpu.VMEM((far, nx - 1, 16, 128), BF16),
+            pltpu.VMEM((far, 16, 128), BF16),
+            pltpu.VMEM((far, 16, 128), BF16),
             dma((5,)), dma, dma((2,)), dma((2, nz)),
             dma((3,)), dma((3,)),
-            dma, dma((nz - 1,)), dma, dma((nz - 1,)), dma, dma,
+            dma, dma((nz - 1,)), dma, dma((nz - 1 - far,)), dma, dma,
+            dma, dma((far,)), dma, dma,
         ],
         compiler_params=pltpu.CompilerParams(
             collective_id=0, has_side_effects=True, vmem_limit_bytes=40 * 1024 * 1024

time: 41.5 us -> 43.1 us (1.039)
  Pallas kernels: 40.7 us -> 42.3 us
    pallas_call x1, Pallas kernels: 40.7 us -> 42.3 us  [local(): pl.pallas_call(functools.partial(kernel, (nz, nx, ny)), out_shape=jax.Sha...]
where the time goes in v7:
time: 43.1 us; the launch traced here: 42.9 us
  Pallas kernels  42.3 us (98%)
  local copies, waits for them, and re-layouts  0.6 us (1%)
    pallas_call x1, Pallas kernels, local(): pl.pallas_call(functools.partial(kernel, (nz, nx, ny)), out_shape=jax.Sha...  42.3 us

profile of v7, /device:TPU:1, one launch (start us, length us, event | category | flops | bytes accessed | tf_op | source)
XLA Modules:
  0.0 42.9 jit_solution(18244678956454535479)
XLA Ops:
  0.0 42.3 %shard_map.64 = f32[16,128]{1,0:T(8,128)S(1)} custom-call(bf16[2,3,8,8192]{3,2,1,0:T(8,128)(2,1)} %fields.1, f32[16,128]{1,0:T(8,128)} %bitcast.11, s32[1,128]{1,0:T(1,128)} %bitcast.14, s32[3,128]{1,0:T(4,128)} %bitcast.12, s32[1,128]{1,0:T(1,128)} %bitcast.15, s32[2,128]{1,0:T(2,128)} %bitcast.13), custom_call_target="tpu_custom_call" | custom-call | tf_op jit(solution)/shard_map/pallas_call | solution.py:372
  42.3 0.6 %copy.9 = f32[8,2,1,128]{3,2,1,0:T(1,128)} copy(f32[8,2,1,128]{3,2,1,0:T(1,128)S(1)} %bitcast.10) | data formatting | bytes 16384

commit v8 on v4

--- a/solution.py
+++ b/solution.py
@@ -31,6 +31,10 @@
 
 def dot_nt(left, right):
     return lax.dot_general(left, right, (((1,), (1,)), ((), ())), preferred_element_type=F32)
+
+
+def far_first(count):
+    return sorted(range(1, count), key=lambda d: -min(d, count - d))
 
 
 def drain(ref, sem):
@@ -61,6 +65,34 @@
     x = p // 2
     core = p % 2
 
+    def line_peer(d):
+        return {"elec": z * lines + (p + d) % lines}
+
+    def z_peer(d):
+        return {"elec": ((z + d) % nz) * lines + p}
+
+    def chip_peer(dz, dx):
+        return {"elec": ((z + dz) % nz) * lines + ((x + dx) % nx) * 2 + core}
+
+    def y_peer(d):
+        return {"cell": (cell + d) % ny}
+
+    core_peer = {"elec": z * lines + x * 2 + 1 - core}
+    next_peer = {"elec": (elec + 1) % groups}
+    prev_peer = {"elec": (elec + groups - 1) % groups}
+
+    if groups < 64:
+        b_buf[...] = jnp.zeros_like(b_buf)
+    barrier = pltpu.get_barrier_semaphore()
+    peers = (
+        [y_peer(d) for d in far_first(ny)]
+        + [chip_peer(dz, dx) for dz in far_first(nz) for dx in range(nx)]
+        + [line_peer(d) for d in far_first(lines)]
+        + [next_peer, prev_peer]
+    )
+    for peer in peers:
+        pl.semaphore_signal(barrier, inc=1, device_id=peer, device_id_type=pl.DeviceIdType.MESH)
+
     inputs = [
         pltpu.make_async_copy(source, target, in_sem.at[number])
         for number, (source, target) in enumerate(
@@ -69,34 +101,6 @@
     ]
     for copy in inputs:
         copy.start()
-
-    def line_peer(d):
-        return {"elec": z * lines + (p + d) % lines}
-
-    def z_peer(d):
-        return {"elec": ((z + d) % nz) * lines + p}
-
-    def chip_peer(dz, dx):
-        return {"elec": ((z + dz) % nz) * lines + ((x + dx) % nx) * 2 + core}
-
-    def y_peer(d):
-        return {"cell": (cell + d) % ny}
-
-    core_peer = {"elec": z * lines + x * 2 + 1 - core}
-    next_peer = {"elec": (elec + 1) % groups}
-    prev_peer = {"elec": (elec + groups - 1) % groups}
-
-    if groups < 64:
-        b_buf[...] = jnp.zeros_like(b_buf)
-    barrier = pltpu.get_barrier_semaphore()
-    peers = (
-        [line_peer(d) for d in range(1, lines)]
-        + [chip_peer(dz, dx) for dz in range(1, nz) for dx in range(nx)]
-        + [y_peer(d) for d in range(1, ny)]
-        + [next_peer, prev_peer]
-    )
-    for peer in peers:
-        pl.semaphore_signal(barrier, inc=1, device_id=peer, device_id_type=pl.DeviceIdType.MESH)
 
     own_copy = pltpu.make_async_copy(fields, own, own_sem)
     own_copy.start()
@@ -154,7 +158,7 @@
 
     pl.semaphore_wait(barrier, len(peers))
 
-    for d in range(1, lines):
+    for d in far_first(lines):
         send(slots.at[(p + d) % lines], a_buf.at[pl.ds((d - 1) * nz, nz)],
              stage_send_sem.at[0], stage_recv_sem.at[0], line_peer(d))
     for s in range(0, halo_ends[0]):
@@ -165,7 +169,7 @@
     drain(arrived, stage_recv_sem.at[0])
     for to in range(nz):
         b_send[to] = a_buf[pl.ds(to, lines, stride=nz), :]
-    for d in range(1, nz):
+    for d in far_first(nz):
         send(b_send.at[(z + d) % nz], b_buf.at[pl.ds((d - 1) * lines, lines)],
              stage_send_sem.at[1], stage_recv_sem.at[1], z_peer(d))
     for s in range(halo_ends[0], halo_ends[1]):
@@ -194,7 +198,7 @@
         for piece in split3(terms[half])[::-1]:
             band = band + dot_nt(columns[half], piece)
     c_send[...] = band
-    for d in range(1, ny):
+    for d in far_first(ny):
         send(c_send, c_buf.at[d - 1], stage_send_sem.at[2], stage_recv_sem.at[2], y_peer(d))
     for s in range(halo_ends[1], nz):
         send_halo(s)

time: 41.5 us -> 40.3 us (0.971)
  Pallas kernels: 40.7 us -> 39.6 us
    pallas_call x1, Pallas kernels: 40.7 us -> 39.6 us  [local(): pl.pallas_call(functools.partial(kernel, (nz, nx, ny)), out_shape=jax.Sha...]
where the time goes in v8:
time: 40.3 us; the launch traced here: 40.2 us
  Pallas kernels  39.6 us (98%)
  local copies, waits for them, and re-layouts  0.6 us (1%)
    pallas_call x1, Pallas kernels, local(): pl.pallas_call(functools.partial(kernel, (nz, nx, ny)), out_shape=jax.Sha...  39.6 us

profile of v8, /device:TPU:1, one launch (start us, length us, event | category | flops | bytes accessed | tf_op | source)
XLA Modules:
  0.0 40.2 jit_solution(16682900611267153990)
XLA Ops:
  0.0 39.6 %shard_map.64 = f32[16,128]{1,0:T(8,128)S(1)} custom-call(bf16[2,3,8,8192]{3,2,1,0:T(8,128)(2,1)} %fields.1, f32[16,128]{1,0:T(8,128)} %bitcast.11, s32[1,128]{1,0:T(1,128)} %bitcast.14, s32[3,128]{1,0:T(4,128)} %bitcast.12, s32[1,128]{1,0:T(1,128)} %bitcast.15, s32[2,128]{1,0:T(2,128)} %bitcast.13), custom_call_target="tpu_custom_call" | custom-call | tf_op jit(solution)/shard_map/pallas_call | solution.py:332
  39.6 0.6 %copy.9 = f32[8,2,1,128]{3,2,1,0:T(1,128)} copy(f32[8,2,1,128]{3,2,1,0:T(1,128)S(1)} %bitcast.10) | data formatting | bytes 16384

commit v9 on v8

--- a/solution.py
+++ b/solution.py
@@ -57,7 +57,7 @@
     lines = 2 * nx
     groups = nz * lines
     quads = resid.shape[1]
-    halo_ends = (0, 3 * nz // 8)
+    halo_ends = (0, nz // 4)
     elec = lax.axis_index("elec")
     cell = lax.axis_index("cell")
     z = elec // lines

time: 40.3 us -> 40.3 us (level)
  no operation moved by 1% of the time
where the time goes in v9:
time: 40.3 us; the launch traced here: 40.2 us
  Pallas kernels  39.6 us (98%)
  local copies, waits for them, and re-layouts  0.6 us (1%)
    pallas_call x1, Pallas kernels, local(): pl.pallas_call(functools.partial(kernel, (nz, nx, ny)), out_shape=jax.Sha...  39.6 us

profile of v9, /device:TPU:1, one launch (start us, length us, event | category | flops | bytes accessed | tf_op | source)
XLA Modules:
  0.0 40.2 jit_solution(2267227183074760218)
XLA Ops:
  0.0 39.6 %shard_map.64 = f32[16,128]{1,0:T(8,128)S(1)} custom-call(bf16[2,3,8,8192]{3,2,1,0:T(8,128)(2,1)} %fields.1, f32[16,128]{1,0:T(8,128)} %bitcast.11, s32[1,128]{1,0:T(1,128)} %bitcast.14, s32[3,128]{1,0:T(4,128)} %bitcast.12, s32[1,128]{1,0:T(1,128)} %bitcast.15, s32[2,128]{1,0:T(2,128)} %bitcast.13), custom_call_target="tpu_custom_call" | custom-call | tf_op jit(solution)/shard_map/pallas_call | solution.py:332
  39.6 0.6 %copy.9 = f32[8,2,1,128]{3,2,1,0:T(1,128)} copy(f32[8,2,1,128]{3,2,1,0:T(1,128)S(1)} %bitcast.10) | data formatting | bytes 16384

commit v10 on v9

--- a/solution.py
+++ b/solution.py
@@ -65,6 +65,15 @@
     x = p // 2
     core = p % 2
 
+    inputs = [
+        pltpu.make_async_copy(source, target, in_sem.at[number])
+        for number, (source, target) in enumerate(
+            zip((resid_in, group_in, offs_in, bstep_in, sides_in), (resid, group, offs, bstep, sides))
+        )
+    ]
+    for copy in inputs:
+        copy.start()
+
     def line_peer(d):
         return {"elec": z * lines + (p + d) % lines}
 
@@ -92,15 +101,6 @@
     )
     for peer in peers:
         pl.semaphore_signal(barrier, inc=1, device_id=peer, device_id_type=pl.DeviceIdType.MESH)
-
-    inputs = [
-        pltpu.make_async_copy(source, target, in_sem.at[number])
-        for number, (source, target) in enumerate(
-            zip((resid_in, group_in, offs_in, bstep_in, sides_in), (resid, group, offs, bstep, sides))
-        )
-    ]
-    for copy in inputs:
-        copy.start()
 
     own_copy = pltpu.make_async_copy(fields, own, own_sem)
     own_copy.start()

time: 40.3 us -> 40.3 us (level)
  no operation moved by 1% of the time
where the time goes in v10:
time: 40.3 us; the launch traced here: 40.2 us
  Pallas kernels  39.6 us (98%)
  local copies, waits for them, and re-layouts  0.6 us (1%)
    pallas_call x1, Pallas kernels, local(): pl.pallas_call(functools.partial(kernel, (nz, nx, ny)), out_shape=jax.Sha...  39.6 us

profile of v10, /device:TPU:1, one launch (start us, length us, event | category | flops | bytes accessed | tf_op | source)
XLA Modules:
  0.0 40.2 jit_solution(536422622390382792)
XLA Ops:
  0.0 39.6 %shard_map.64 = f32[16,128]{1,0:T(8,128)S(1)} custom-call(bf16[2,3,8,8192]{3,2,1,0:T(8,128)(2,1)} %fields.1, f32[16,128]{1,0:T(8,128)} %bitcast.11, s32[1,128]{1,0:T(1,128)} %bitcast.14, s32[3,128]{1,0:T(4,128)} %bitcast.12, s32[1,128]{1,0:T(1,128)} %bitcast.15, s32[2,128]{1,0:T(2,128)} %bitcast.13), custom_call_target="tpu_custom_call" | custom-call | tf_op jit(solution)/shard_map/pallas_call | solution.py:332
  39.6 0.6 %copy.9 = f32[8,2,1,128]{3,2,1,0:T(1,128)} copy(f32[8,2,1,128]{3,2,1,0:T(1,128)S(1)} %bitcast.10) | data formatting | bytes 16384

commit v11 on v10

--- a/solution.py
+++ b/solution.py
@@ -47,7 +47,7 @@
     out,
     resid, group, offs, bstep, sides,
     own, low, high,
-    slots, a_buf, b_send, b_buf, c_send, c_buf, weights,
+    slots, b_buf, c_send, c_buf, weights,
     part, core_recv, sums, rounded, shares,
     in_sem, own_sem, halo_send_sem, halo_recv_sem,
     stage_send_sem, stage_recv_sem,
@@ -80,6 +80,9 @@
     def z_peer(d):
         return {"elec": ((z + d) % nz) * lines + p}
 
+    def plane_peer(dz, dp):
+        return {"elec": ((z + dz) % nz) * lines + (p + dp) % lines}
+
     def chip_peer(dz, dx):
         return {"elec": ((z + dz) % nz) * lines + ((x + dx) % nx) * 2 + core}
 
@@ -93,10 +96,10 @@
     if groups < 64:
         b_buf[...] = jnp.zeros_like(b_buf)
     barrier = pltpu.get_barrier_semaphore()
+    plane = [(dz, dp) for dz in far_first(nz) + [0] for dp in far_first(lines) + [0]][:-1]
     peers = (
         [y_peer(d) for d in far_first(ny)]
-        + [chip_peer(dz, dx) for dz in far_first(nz) for dx in range(nx)]
-        + [line_peer(d) for d in far_first(lines)]
+        + [plane_peer(dz, dp) for dz, dp in plane]
         + [next_peer, prev_peer]
     )
     for peer in peers:
@@ -153,31 +156,22 @@
     )
     named = member.astype(BF16)
     sorted_rows = sum(dot_nt(named, piece) for piece in split3(entries)[::-1])
-    for line in range(lines):
-        slots[line] = sorted_rows[line * nz:(line + 1) * nz, :]
+    slots[...] = sorted_rows.reshape(groups, 1, 128)
 
     pl.semaphore_wait(barrier, len(peers))
 
-    for d in far_first(lines):
-        send(slots.at[(p + d) % lines], a_buf.at[pl.ds((d - 1) * nz, nz)],
-             stage_send_sem.at[0], stage_recv_sem.at[0], line_peer(d))
-    for s in range(0, halo_ends[0]):
-        send_halo(s)
-    a_buf[pl.ds((lines - 1) * nz, nz), :] = slots[p]
-    own_copy.wait()
-    arrived = a_buf.at[pl.ds(0, (lines - 1) * nz)]
-    drain(arrived, stage_recv_sem.at[0])
-    for to in range(nz):
-        b_send[to] = a_buf[pl.ds(to, lines, stride=nz), :]
-    for d in far_first(nz):
-        send(b_send.at[(z + d) % nz], b_buf.at[pl.ds((d - 1) * lines, lines)],
-             stage_send_sem.at[1], stage_recv_sem.at[1], z_peer(d))
+    for dz, dp in plane:
+        to = (p + dp) % lines * nz + (z + dz) % nz
+        send(slots.at[to], b_buf.at[dz * lines + dp - 1],
+             stage_send_sem.at[0], stage_recv_sem.at[0], plane_peer(dz, dp))
     for s in range(halo_ends[0], halo_ends[1]):
         send_halo(s)
-    b_buf[pl.ds((nz - 1) * lines, lines), :] = b_send[z]
-    drain(b_buf.at[pl.ds(0, (nz - 1) * lines)], stage_recv_sem.at[1])
-
-    received = b_buf[...]
+    b_buf[groups - 1] = slots[p * nz + z]
+    own_copy.wait()
+    arrived = b_buf.at[pl.ds(0, groups - 1)]
+    drain(arrived, stage_recv_sem.at[0])
+
+    received = b_buf[...].reshape(64, 128)
     both = jnp.concatenate([received, pltpu.roll(received, 64, 1)], axis=0)
     turned = both.T
     terms = []
@@ -199,10 +193,10 @@
             band = band + dot_nt(columns[half], piece)
     c_send[...] = band
     for d in far_first(ny):
-        send(c_send, c_buf.at[d - 1], stage_send_sem.at[2], stage_recv_sem.at[2], y_peer(d))
+        send(c_send, c_buf.at[d - 1], stage_send_sem.at[1], stage_recv_sem.at[1], y_peer(d))
     for s in range(halo_ends[1], nz):
         send_halo(s)
-    drain(c_buf, stage_recv_sem.at[2])
+    drain(c_buf, stage_recv_sem.at[1])
     for d in range(ny - 1):
         band = band + c_buf[d]
     band = band.astype(BF16).astype(F32)
@@ -311,8 +305,7 @@
     drain(low, halo_send_sem.at[0])
     drain(high, halo_send_sem.at[1])
     drain(arrived, stage_send_sem.at[0])
-    drain(b_buf.at[pl.ds(0, (nz - 1) * lines)], stage_send_sem.at[1])
-    drain(c_buf, stage_send_sem.at[2])
+    drain(c_buf, stage_send_sem.at[1])
     drain(core_recv, core_send_sem)
     drain(shares.at[pl.ds(0, nz * nx - 1)], share_send_sem)
 
@@ -343,10 +336,8 @@
             pltpu.VMEM(field_shape, BF16),
             pltpu.VMEM(field_shape, BF16),
             pltpu.VMEM(field_shape, BF16),
-            pltpu.VMEM((lines, nz, 128), F32),
-            pltpu.VMEM((groups, 128), F32),
-            pltpu.VMEM((nz, lines, 128), F32),
-            pltpu.VMEM((64, 128), F32),
+            pltpu.VMEM((groups, 1, 128), F32),
+            pltpu.VMEM((64, 1, 128), F32),
             pltpu.VMEM((WINDOW, 128), F32),
             pltpu.VMEM((ny - 1, WINDOW, 128), F32),
             pltpu.VMEM((384, 256), BF16),
@@ -356,7 +347,7 @@
             pltpu.VMEM((nz, nx, 16, 128), BF16),
             pltpu.VMEM((nz * nx, 16, 128), BF16),
             dma((5,)), dma, dma((2,)), dma((2, nz)),
-            dma((3,)), dma((3,)),
+            dma((2,)), dma((2,)),
             dma, dma((nz,)), dma, dma((nz,)),
         ],
         compiler_params=pltpu.CompilerParams(

time: 40.3 us -> 38.3 us (0.950)
  Pallas kernels: 39.6 us -> 37.5 us
    pallas_call x1, Pallas kernels: 39.6 us -> 37.5 us  [local(): pl.pallas_call(functools.partial(kernel, (nz, nx, ny)), out_shape=jax.Sha...]
where the time goes in v11:
time: 38.3 us; the launch traced here: 38.2 us
  Pallas kernels  37.5 us (98%)
  local copies, waits for them, and re-layouts  0.6 us (2%)
    pallas_call x1, Pallas kernels, local(): pl.pallas_call(functools.partial(kernel, (nz, nx, ny)), out_shape=jax.Sha...  37.5 us

profile of v11, /device:TPU:1, one launch (start us, length us, event | category | flops | bytes accessed | tf_op | source)
XLA Modules:
  0.0 38.2 jit_solution(7430270682002479678)
XLA Ops:
  0.0 37.5 %shard_map.64 = f32[16,128]{1,0:T(8,128)S(1)} custom-call(bf16[2,3,8,8192]{3,2,1,0:T(8,128)(2,1)} %fields.1, f32[16,128]{1,0:T(8,128)} %bitcast.11, s32[1,128]{1,0:T(1,128)} %bitcast.14, s32[3,128]{1,0:T(4,128)} %bitcast.12, s32[1,128]{1,0:T(1,128)} %bitcast.15, s32[2,128]{1,0:T(2,128)} %bitcast.13), custom_call_target="tpu_custom_call" | custom-call | tf_op jit(solution)/shard_map/pallas_call | solution.py:325
  37.6 0.6 %copy.9 = f32[8,2,1,128]{3,2,1,0:T(1,128)} copy(f32[8,2,1,128]{3,2,1,0:T(1,128)S(1)} %bitcast.10) | data formatting | bytes 16384

commit v12 on v11

--- a/solution.py
+++ b/solution.py
@@ -279,7 +279,7 @@
         def _():
             share(s, 0)
 
-    core_lag = 2
+    core_lag = 3
 
     def step(s, carry):
         @pl.when(s < nz)

time: 38.3 us -> 38.4 us (level)
  no operation moved by 1% of the time
where the time goes in v12:
time: 38.4 us; the launch traced here: 38.2 us
  Pallas kernels  37.6 us (98%)
  local copies, waits for them, and re-layouts  0.6 us (2%)
    pallas_call x1, Pallas kernels, local(): pl.pallas_call(functools.partial(kernel, (nz, nx, ny)), out_shape=jax.Sha...  37.6 us

profile of v12, /device:TPU:1, one launch (start us, length us, event | category | flops | bytes accessed | tf_op | source)
XLA Modules:
  0.0 38.2 jit_solution(1291375806280267978)
XLA Ops:
  0.0 37.6 %shard_map.64 = f32[16,128]{1,0:T(8,128)S(1)} custom-call(bf16[2,3,8,8192]{3,2,1,0:T(8,128)(2,1)} %fields.1, f32[16,128]{1,0:T(8,128)} %bitcast.11, s32[1,128]{1,0:T(1,128)} %bitcast.14, s32[3,128]{1,0:T(4,128)} %bitcast.12, s32[1,128]{1,0:T(1,128)} %bitcast.15, s32[2,128]{1,0:T(2,128)} %bitcast.13), custom_call_target="tpu_custom_call" | custom-call | tf_op jit(solution)/shard_map/pallas_call | solution.py:325
  37.6 0.6 %copy.9 = f32[8,2,1,128]{3,2,1,0:T(1,128)} copy(f32[8,2,1,128]{3,2,1,0:T(1,128)S(1)} %bitcast.10) | data formatting | bytes 16384
